TPU v7x, 32 devices: a whole 2x2x4 slice. The times are simulated.
32 devices in a mesh: clip: 2 (over x), seq: 16 (over z, y, core).
Axes of the slice: x: 2, y: 2, z: 4, core: 2. Of those that a mesh axis runs over, the one named last changes fastest.
Arguments:
- spatial_saved: bfloat16 [3, 32, 256, 576], P(None, ('clip', 'seq')), parts along dimension 1, may hold values from -48 to 48
- hidden: bfloat16 [32, 256, 1152], P(('clip', 'seq')), parts along dimension 0, may hold values from -6 to 6
- temporal_out_grad: bfloat16 [32, 256, 576], P(('clip', 'seq')), parts along dimension 0, may hold values from -6 to 6
- stream_grad: bfloat16 [32, 256, 1152], P(('clip', 'seq')), parts along dimension 0, may hold values from -6 to 6
- modulation: float32 [1152], replicated, may hold values from -0.5 to 1
- temporal_weights: bfloat16 [1152, 1728], P('seq'), may hold values from -0.1875 to 0.1875
- spatial_weights: bfloat16 [576, 1152], P('seq'), may hold values from -0.25 to 0.25
Outputs:
- hidden_grad: bfloat16 [32, 256, 1152], P(('clip', 'seq')), parts along dimension 0
- spatial_grad: bfloat16 [3, 32, 256, 576], P(None, ('clip', 'seq')), parts along dimension 1
There are 2 independent parts, one for each index of `clip`. A program takes and returns all parts, laid end to end along the dimension named above; an argument that names none is the same for every part. Nothing has to cross between parts.
All inputs are finite; a program needn't handle non-finite values.
Results may differ from a plain program's by a relative error of at most 0.024.
Values may be sent and summed in bfloat16 or wider, within the bound.
No kernel may reach another device: no remote copies, remote signals or barrier semaphores. Data moves between devices by JAX's collectives and lax.ppermute only.
A program may use at most 64 MiB of HBM per device.

v0:
```python
import math
import jax
import jax.numpy as jnp
from jax import lax
from jax.sharding import PartitionSpec as P

HEADS = 8
HD = 72
epsilon = 1e-06


def attend_grad(query, keys, values, grad_o, form):
    key_form = form.replace("l", "m")
    scale = 1.0 / math.sqrt(query.shape[-1])
    scores = (
        jnp.einsum(
            form + "," + key_form + "->bhlm", query, keys, preferred_element_type=jnp.float32
        )
        * scale
    )
    attention = jax.nn.softmax(scores, axis=-1)
    rounded = attention.astype(jnp.bfloat16)
    output = jnp.einsum(
        "bhlm," + key_form + "->" + form, rounded, values, preferred_element_type=jnp.float32
    )
    delta = jnp.einsum(form + "," + form + "->bhl", grad_o.astype(jnp.float32), output)
    spread = jnp.einsum(
        form + "," + key_form + "->bhlm", grad_o, values, preferred_element_type=jnp.float32
    )
    dscore = (attention * (spread - delta[..., None])).astype(jnp.bfloat16)
    grad_query = jnp.einsum(
        "bhlm," + key_form + "->" + form, dscore, keys, preferred_element_type=jnp.float32
    )
    grad_keys = jnp.einsum(
        "bhlm," + form + "->" + key_form, dscore, query, preferred_element_type=jnp.float32
    )
    grad_values = jnp.einsum(
        "bhlm," + form + "->" + key_form, rounded, grad_o, preferred_element_type=jnp.float32
    )
    return (
        (grad_query * scale).astype(jnp.bfloat16),
        (grad_keys * scale).astype(jnp.bfloat16),
        grad_values.astype(jnp.bfloat16),
    )


def split_heads(block):
    return block.reshape(block.shape[:-1] + (HEADS, HD))


def merge_heads(block):
    return block.reshape(block.shape[:-2] + (HEADS * HD,))


def layer_norm(hidden, modulation):
    widened = hidden.astype(jnp.float32)
    mean_value = jnp.mean(widened, axis=-1, keepdims=True)
    centered = widened - mean_value
    inverse = lax.rsqrt(jnp.mean(centered * centered, axis=-1, keepdims=True) + epsilon)
    normal_form = centered * inverse
    normed = (normal_form * (1.0 + modulation)).astype(jnp.bfloat16)
    return (normed, normal_form, inverse)


def norm_back(grad_normed, normal_form, inverse, modulation):
    scaled = grad_normed * (1.0 + modulation)
    return inverse * (
        scaled
        - jnp.mean(scaled, axis=-1, keepdims=True)
        - normal_form * jnp.mean(scaled * normal_form, axis=-1, keepdims=True)
    )


def temporal_backward(projected, grad_patch):
    width = HEADS * HD
    grads = attend_grad(
        split_heads(projected[..., :width]),
        split_heads(projected[..., width : 2 * width]),
        split_heads(projected[..., 2 * width :]),
        split_heads(grad_patch),
        "lbhd",
    )
    return jnp.concatenate([merge_heads(gradient) for gradient in grads], axis=-1)


def shards(
    spatial_saved,
    hidden,
    temporal_out_grad,
    stream_grad,
    modulation,
    temporal_weights,
    spatial_weights,
):
    grad_patch = lax.all_to_all(temporal_out_grad, "seq", split_axis=1, concat_axis=0, tiled=True)
    hidden_patch = lax.all_to_all(hidden, "seq", split_axis=1, concat_axis=0, tiled=True)
    normed, normal_form, inverse = layer_norm(hidden_patch, modulation)
    projected = jnp.einsum(
        "fpd,dc->fpc",
        normed,
        lax.all_gather(temporal_weights, "seq", axis=0, tiled=True),
        preferred_element_type=jnp.float32,
    ).astype(jnp.bfloat16)
    projection_grads = temporal_backward(projected, grad_patch)
    branch = norm_back(
        jnp.einsum(
            "fpc,dc->fpd",
            projection_grads,
            lax.all_gather(temporal_weights, "seq", axis=0, tiled=True),
            preferred_element_type=jnp.float32,
        ),
        normal_form,
        inverse,
        modulation,
    ).astype(jnp.bfloat16)
    branch = lax.all_to_all(branch, "seq", split_axis=0, concat_axis=1, tiled=True)
    branch = lax.optimization_barrier(branch)
    hidden_grad = (stream_grad.astype(jnp.float32) + branch.astype(jnp.float32)).astype(
        jnp.bfloat16
    )
    attention_grad = jnp.einsum(
        "fpd,cd->fpc",
        hidden_grad,
        lax.all_gather(spatial_weights, "seq", axis=0, tiled=True),
        preferred_element_type=jnp.float32,
    ).astype(jnp.bfloat16)
    spatial = attend_grad(
        split_heads(spatial_saved[0]),
        split_heads(spatial_saved[1]),
        split_heads(spatial_saved[2]),
        split_heads(attention_grad),
        "blhd",
    )
    spatial_grad = jnp.stack([merge_heads(gradient) for gradient in spatial])
    return (hidden_grad, spatial_grad)


def solution(mesh):
    return jax.shard_map(
        shards,
        mesh=mesh,
        in_specs=(
            P(None, ("clip", "seq"), None, None),
            P(("clip", "seq"), None, None),
            P(("clip", "seq"), None, None),
            P(("clip", "seq"), None, None),
            P(),
            P("seq", None),
            P("seq", None),
        ),
        out_specs=(P(("clip", "seq"), None, None), P(None, ("clip", "seq"), None, None)),
        check_vma=False,
    )
```

profile of v0, /device:TPU:0, one launch (start us, length us, event | category | flops | bytes accessed | tf_op | source)
XLA Modules:
  0.0 136.8 jit_solution(4414544214536378165)
XLA Ops:
  7.2 0.0 all-gather.4.cloned.1.call-start
  7.2 0.7 all-gather.4.cloned.1.call-update
  7.9 1.4 %copy.61 = bf16[1,256,576]{2,0,1:T(2,128)(2,1)S(1)} copy(bf16[1,256,576]{1,2,0:T(8,128)(2,1)} %param.9) | data formatting | bytes 589824 | tf_op args[2]
  9.3 0.0 copy-start.3
  9.3 0.5 broadcast.94
  9.9 2.7 %reduce.13 = bf16[256,576]{1,0:T(8,128)(2,1)S(1)} reduce(bf16[256,1,576]{2,1,0:T(2,128)(2,1)S(1)} %bitcast.105, bf16[]{:T(256)} %broadcast.94), dimensions={1}, to_apply=%bitcast.75.reduce_sub_computation | reduce | bytes 589826
  12.6 1.1 reshape.177
  13.7 7.4 %all-to-all-start.1 = ((bf16[16,2,4608]{2,1,0:T(2,128)(2,1)}), bf16[16,2,4608]{2,1,0:T(2,128)(2,1)S(1)}, u32[]{:S(2)}, u32[]{:S(2)}) async-start(bf16[16,2,4608]{2,1,0:T(2,128)(2,1)} %reshape.177), calls=%async_computation.1 | async-start | bytes 589824 | tf_op jit(solution)/shard_map/all_to_all | solution.py:95
  21.1 0.9 copy.134
  22.0 4.2 %reduce.12 = bf16[256,1152]{1,0:T(8,128)(2,1)S(1)} reduce(bf16[256,1,1152]{2,1,0:T(2,128)(2,1)S(1)} %bitcast.101, bf16[]{:T(256)} %broadcast.94), dimensions={1}, to_apply=%bitcast.97.reduce_sub_computation | reduce | bytes 1179650
  26.2 0.9 reshape.175
  27.2 9.1 %all-to-all-done.1 = bf16[16,2,4608]{2,1,0:T(2,128)(2,1)S(1)} async-done(((bf16[16,2,4608]{2,1,0:T(2,128)(2,1)}), bf16[16,2,4608]{2,1,0:T(2,128)(2,1)S(1)}, u32[]{:S(2)}, u32[]{:S(2)}) %all-to-all-start.1) | async-done | bytes 294944 | tf_op jit(solution)/shard_map/all_to_all | solution.py:95
  36.3 4.8 %all-to-all-start = ((bf16[16,2,9216]{2,1,0:T(2,128)(2,1)}), bf16[16,2,9216]{2,1,0:T(2,128)(2,1)S(1)}, u32[]{:S(2)}, u32[]{:S(2)}) async-start(bf16[16,2,9216]{2,1,0:T(2,128)(2,1)} %reshape.175), calls=%async_computation | async-start | bytes 1179648 | tf_op jit(solution)/shard_map/all_to_all | solution.py:96
  41.1 0.2 all-gather.6.cloned.1.call-start
  41.3 0.5 all-gather.6.cloned.1.call-update
  41.9 0.6 reshape.178
  42.4 1.8 %bitcast_reduce_fusion = bf16[256,576]{1,0:T(8,128)(2,1)S(1)} fusion(bf16[256,1,576]{2,1,0:T(2,128)(2,1)S(1)} %reshape.178), kind=kLoop, calls=%fused_computation.78 | loop fusion | bytes 589824 | tf_op jit(solution)/shard_map/all_to_all | solution.py:95
  44.3 0.6 reshape.154
  44.8 19.4 %all-to-all-done = bf16[16,2,9216]{2,1,0:T(2,128)(2,1)S(1)} async-done(((bf16[16,2,9216]{2,1,0:T(2,128)(2,1)}), bf16[16,2,9216]{2,1,0:T(2,128)(2,1)S(1)}, u32[]{:S(2)}, u32[]{:S(2)}) %all-to-all-start) | async-done | bytes 589856 | tf_op jit(solution)/shard_map/all_to_all | solution.py:96
  64.3 0.5 reshape.176
  64.7 0.1 fusion.54
  64.9 0.3 multiply_reduce_fusion.2
  65.2 0.1 div.33
  65.3 0.1 copy_convert_fusion
  65.4 0.1 rsqrt.12
  65.4 10.7 %all-gather.4.cloned.1.call-done = bf16[1152,1728]{1,0:T(8,128)(2,1)} async-done(((bf16[72,1728]{1,0:T(8,128)(2,1)}), bf16[1152,1728]{1,0:T(8,128)(2,1)}) %all-gather.4.cloned.1.call-update) | async-done | bytes 3981328 | tf_op jit(solution)/shard_map/all_gather | solution.py:101
  76.1 3.6 %fusion.9 = bf16[16,16,1728]{2,1,0:T(8,128)(2,1)S(1)} fusion(bf16[1152,1728]{1,0:T(8,128)(2,1)} %all-gather.4.cloned.1.call-done, f32[16,16,1152]{2,1,0:T(8,128)S(1)} %bitcast.102, f32[1152]{0:T(1024)S(1)} %broadcast_add_fusion, f32[16,16]{1,0:T(8,128)S(1)} %div.33, f32[16,16]{1,0:T(8,128)S(1)} %rsqrt.12), kind=kOutput, calls=%fused_computation.7 | convolution fusion | flops 1020837888 | bytes 6052352 | tf_op jit(solution)/shard_map/fpd,dc->fpc/dot_general | solution.py:98
  79.7 0.2 fusion.58
  79.9 0.6 reshape.151
  80.5 0.6 reshape.152
  81.0 1.4 reshape.153
  82.4 2.0 %fusion.60 = (f32[16,8,16]{2,1,0:T(8,128)S(1)}, f32[16,8,16,16]{2,3,1,0:T(8,128)}) fusion(bf16[16,16,8,72]{3,2,1,0:T(8,128)(2,1)S(1)} %reshape.151, bf16[16,16,8,72]{3,2,1,0:T(8,128)(2,1)S(1)} %reshape.152), kind=kOutput, calls=%fused_computation.75 | convolution fusion | flops 4816911 | bytes 729088 | tf_op jit(solution)/shard_map/sub | solution.py:21
  84.4 2.7 %fusion.22 = bf16[16,16,8,72]{3,0,2,1:T(8,128)(2,1)} fusion(bf16[16,16,8,72]{3,2,1,0:T(8,128)(2,1)S(1)} %reshape.154, f32[16,8,16,16]{2,3,1,0:T(8,128)} %get-tuple-element.11, f32[16,8,16]{2,1,0:T(8,128)S(1)} %get-tuple-element.10), kind=kOutput, calls=%fused_computation.30 | convolution fusion | flops 4931584 | bytes 729088 | tf_op jit(solution)/shard_map/bhlm,lbhd->mbhd/dot_general | solution.py:37
  87.1 0.5 convolution_bitcast_fusion
  87.6 0.5 multiply_reduce_fusion.3
  88.1 0.1 copy.85
  88.2 2.0 %fusion.17 = bf16[16,8,16,16]{2,3,1,0:T(8,128)(2,1)S(1)} fusion(f32[16,8,16]{2,1,0:T(8,128)S(1)} %copy.85, bf16[16,16,8,72]{3,2,1,0:T(8,128)(2,1)S(1)} %reshape.154, bf16[16,16,8,72]{3,2,1,0:T(8,128)(2,1)S(1)} %copy-done.6, f32[16,8,16,16]{2,3,1,0:T(8,128)} %get-tuple-element.11, f32[16,8,16]{2,1,0:T(8,128)} %copy-done.11), kind=kOutput, calls=%fused_computation.21 | convolution fusion | flops 4849664 | bytes 802816 | tf_op jit(solution)/shard_map/lbhd,mbhd->bhlm/dot_general | solution.py:27
  90.2 0.4 fusion.20
  90.6 0.5 fusion.21
  91.1 0.5 copy-done.5
  91.7 0.1 copy.72
  91.8 0.4 reshape.157
  92.2 0.1 copy.70
  92.3 0.4 reshape.156
  92.7 0.1 copy.68
  92.8 0.4 reshape.155
  93.2 1.2 concatenate.3
  94.4 3.9 %fusion.57 = (f32[16,16]{1,0:T(8,128)S(1)}, f32[16,16]{1,0:T(8,128)S(1)}, f32[16,16,1152]{2,1,0:T(8,128)S(1)}) fusion(f32[16,16]{1,0:T(8,128)S(1)} %rsqrt.12, f32[16,16,1152]{2,1,0:T(8,128)S(1)} %bitcast.103, f32[16,16]{1,0:T(8,128)S(1)} %div.33, f32[1152]{0:T(1024)S(1)} %broadcast_add_fusion, bf16[16,16,1728]{2,1,0:T(8,128)(2,1)} %concatenate.3, ...), kind=kOutput, calls=%fused_computation.72 | convolution fusion | flops 1020984832 | bytes 7234048 | tf_op jit(solution)/shard_map/fpc,dc->fpd/dot_general | solution.py:106
  98.4 1.2 multiply_convert_fusion.1
  99.6 3.8 %all-to-all-start.2 = ((bf16[16,16,1152]{2,1,0:T(8,128)(2,1)}), bf16[16,16,1152]{2,1,0:T(8,128)(2,1)S(1)}, u32[]{:S(2)}, u32[]{:S(2)}) async-start(bf16[16,16,1152]{2,1,0:T(8,128)(2,1)} %multiply_convert_fusion.1), calls=%async_computation.2 | async-start | bytes 1179648 | tf_op jit(solution)/shard_map/all_to_all | solution.py:116
  103.4 0.8 fusion.59
  104.2 2.2 %fusion.65 = (f32[8,256]{1,0:T(8,128)S(1)}, f32[8,256,256]{1,2,0:T(8,128)}) fusion(bf16[256,8,72]{0,2,1:T(8,128)(2,1)S(1)} %bitcast.107, bf16[256,8,72]{0,2,1:T(8,128)(2,1)S(1)} %bitcast.109), kind=kOutput, calls=%fused_computation.76 | convolution fusion | flops 77070592 | bytes 2695168 | tf_op jit(solution)/shard_map/sub | solution.py:21
  106.4 1.8 %fusion.27 = bf16[8,256,256]{1,2,0:T(8,128)(2,1)S(1)} fusion(f32[8,256,256]{1,2,0:T(8,128)} %get-tuple-element.14, f32[8,256]{1,0:T(8,128)S(1)} %get-tuple-element.13), kind=kLoop, calls=%fused_computation.46 | loop fusion | flops 1048576 | bytes 3153920 | tf_op jit(solution)/shard_map/convert_element_type | solution.py:22
  108.2 13.7 %all-gather.6.cloned.1.call-done = bf16[16,36,1152]{2,1,0:T(8,128)(2,1)} async-done(((bf16[1,36,1152]{2,1,0:T(8,128)(2,1)}), bf16[16,36,1152]{2,1,0:T(8,128)(2,1)}) %all-gather.6.cloned.1.call-update) | async-done | bytes 1327120 | tf_op jit(solution)/shard_map/all_gather | solution.py:124
  121.9 2.2 %reshape.166 = bf16[576,1152]{1,0:T(8,128)(2,1)S(1)} reshape(bf16[16,36,1152]{2,1,0:T(8,128)(2,1)} %all-gather.6.cloned.1.call-done) | data formatting | bytes 2654208
  124.2 1.2 add_convert_fusion
  125.4 0.6 convolution_convert_fusion.1
  126.1 0.3 fusion.25
  126.4 0.8 copy-done
  127.2 0.5 multiply_convert_fusion
  127.7 0.3 fusion.23
  128.1 0.5 fusion.24
  128.5 0.4 convolution_convert_fusion.2
  129.0 1.0 pad_maximum_fusion
  (26 shorter events, 0.1 us)
Async XLA Ops:
  7.2 69.0 %all-gather.4.cloned.1.call-start = ((), (), s32[]{:S(2)}) async-start(), calls=%async_computation.3 | async-start | bytes 4386816 | tf_op jit(solution)/shard_map/all_gather | solution.py:101
  9.3 11.7 %copy-start.3 = (bf16[1,256,1152]{2,1,0:T(8,128)(2,1)S(1)}, bf16[1,256,1152]{2,1,0:T(8,128)(2,1)}, u32[]{:S(2)}) copy-start(bf16[1,256,1152]{2,1,0:T(8,128)(2,1)} %param.8) | copy-start | bytes 1769476
  13.7 22.6 %all-to-all-start.1 = ((bf16[16,2,4608]{2,1,0:T(2,128)(2,1)}), bf16[16,2,4608]{2,1,0:T(2,128)(2,1)S(1)}, u32[]{:S(2)}, u32[]{:S(2)}) async-start(bf16[16,2,4608]{2,1,0:T(2,128)(2,1)} %reshape.177), calls=%async_computation.1 | async-start | bytes 589824 | tf_op jit(solution)/shard_map/all_to_all | solution.py:95
  26.2 15.6 %copy-start.9 = (f32[1152]{0:T(1024)S(1)}, f32[1152]{0:T(1024)}, u32[]{:S(2)}) copy-start(f32[1152]{0:T(1024)} %param.11) | copy-start | bytes 13828
  36.3 28.0 %all-to-all-start = ((bf16[16,2,9216]{2,1,0:T(2,128)(2,1)}), bf16[16,2,9216]{2,1,0:T(2,128)(2,1)S(1)}, u32[]{:S(2)}, u32[]{:S(2)}) async-start(bf16[16,2,9216]{2,1,0:T(2,128)(2,1)} %reshape.175), calls=%async_computation | async-start | bytes 1179648 | tf_op jit(solution)/shard_map/all_to_all | solution.py:96
  41.1 80.8 %all-gather.6.cloned.1.call-start = ((), (), s32[]{:S(2)}) async-start(), calls=%async_computation.4 | async-start | bytes 1566720 | tf_op jit(solution)/shard_map/all_gather | solution.py:124
  84.4 2.7 %copy-start.11 = (f32[16,8,16]{2,1,0:T(8,128)}, f32[16,8,16]{2,1,0:T(8,128)S(1)}, u32[]{:S(2)}) copy-start(f32[16,8,16]{2,1,0:T(8,128)S(1)} %get-tuple-element.10) | copy-start | bytes 24580
  84.4 2.7 %copy-start.6 = (bf16[16,16,8,72]{3,2,1,0:T(8,128)(2,1)S(1)}, bf16[16,16,8,72]{3,2,1,0:T(8,128)(2,1)}, u32[]{:S(2)}) copy-start(bf16[16,16,8,72]{3,2,1,0:T(8,128)(2,1)} %reshape.153) | copy-start | bytes 884740
  84.4 2.7 %copy-start.10 = (f32[16,8,16,16]{2,3,1,0:T(8,128)S(1)}, f32[16,8,16,16]{2,3,1,0:T(8,128)}, u32[]{:S(2)}) copy-start(f32[16,8,16,16]{2,3,1,0:T(8,128)} %get-tuple-element.11) | copy-start | bytes 393220
  90.6 1.0 copy-start.5
  99.6 3.8 %copy-start.2 = (bf16[3,1,256,576]{2,3,1,0:T(8,128)(2,1)S(1)}, bf16[3,1,256,576]{2,3,1,0:T(8,128)(2,1)}, u32[]{:S(2)}) copy-start(bf16[3,1,256,576]{2,3,1,0:T(8,128)(2,1)} %param.7) | copy-start | bytes 2654212
  99.6 24.6 %all-to-all-start.2 = ((bf16[16,16,1152]{2,1,0:T(8,128)(2,1)}), bf16[16,16,1152]{2,1,0:T(8,128)(2,1)S(1)}, u32[]{:S(2)}, u32[]{:S(2)}) async-start(bf16[16,16,1152]{2,1,0:T(8,128)(2,1)} %multiply_convert_fusion.1), calls=%async_computation.2 | async-start | bytes 1179648 | tf_op jit(solution)/shard_map/all_to_all | solution.py:116
  106.4 1.8 %copy-start.7 = (f32[8,256]{1,0:T(8,128)}, f32[8,256]{1,0:T(8,128)S(1)}, u32[]{:S(2)}) copy-start(f32[8,256]{1,0:T(8,128)S(1)} %get-tuple-element.13) | copy-start | bytes 24580
  124.2 1.9 %copy-start.1 = (bf16[1,1,256,576]{2,3,1,0:T(8,128)(2,1)S(1)}, bf16[1,1,256,576]{2,3,1,0:T(8,128)(2,1)}, u32[]{:S(2)}) copy-start(bf16[1,1,256,576]{2,3,1,0:T(8,128)(2,1)} %get-tuple-element.7) | copy-start | bytes 884740
  125.4 1.0 copy-start.4
  125.4 1.8 %copy-start = (f32[8,256,256]{1,2,0:T(8,128)S(1)}, f32[8,256,256]{1,2,0:T(8,128)}, u32[]{:S(2)}) copy-start(f32[8,256,256]{1,2,0:T(8,128)} %get-tuple-element.14) | copy-start | bytes 6291460
  126.0 1.2 copy-start.8
Sparse Core Ops, SparseCore 0:
  10.3 65.7 all-gather.3
  78.3 43.5 all-gather.5
where the time goes:
time: 138 us; the launch traced here: 137 us
  waiting for transfers between devices  54.1 us (39%)
  matrix products  20.4 us (15%)
  local copies, waits for them, and re-layouts  18.4 us (13%)
  starting transfers between devices  16.2 us (12%)
  between operations  14.4 us (10%)
  other arithmetic  13.2 us (10%)
    all_to_all x1, waiting for transfers between devices, shards(): lax.all_to_all(hidden, 'seq', split_axis=1, concat_axis=0, tiled=True)  19.4 us
    all_gather x1, waiting for transfers between devices, shards(): lax.all_gather(spatial_weights, 'seq', axis=0, tiled=True)  13.7 us
    all_gather x1, waiting for transfers between devices, shards(): lax.all_gather(temporal_weights, 'seq', axis=0, tiled=True)  10.7 us
    unnamed x32, local copies, waits for them, and re-layouts  9.62 us
    all_to_all x1, waiting for transfers between devices, shards(): lax.all_to_all(temporal_out_grad, 'seq', split_axis=1, concat_axis=0, til...  9.12 us
    unnamed x3, other arithmetic  7.44 us
    all_to_all x1, starting transfers between devices, shards(): lax.all_to_all(temporal_out_grad, 'seq', split_axis=1, concat_axis=0, til...  7.39 us
    all_to_all x1, starting transfers between devices, shards(): lax.all_to_all(hidden, 'seq', split_axis=1, concat_axis=0, tiled=True)  4.79 us
  transfers between devices with their start and end apart: 5, of which 4 were waited for; matrix products, arithmetic and copies ran while one was open for 33% of the time, Pallas kernels for 0%

commit v1 on v0

--- a/solution.py
+++ b/solution.py
@@ -3,6 +3,7 @@
 import jax.numpy as jnp
 from jax import lax
 from jax.sharding import PartitionSpec as P
+from jax.lax import axis_index, axis_size, ppermute
 
 HEADS = 8
 HD = 72
@@ -93,7 +94,22 @@
     spatial_weights,
 ):
     grad_patch = lax.all_to_all(temporal_out_grad, "seq", split_axis=1, concat_axis=0, tiled=True)
-    hidden_patch = lax.all_to_all(hidden, "seq", split_axis=1, concat_axis=0, tiled=True)
+    shaped = axis_size("seq")
+    u1 = axis_index("seq")
+    part_next, odd = (shaped, u1)
+    main = hidden.shape[1] // part_next
+    e_now = list(hidden.shape)
+    e_now[1] = main
+    built = e_now[0]
+    e_now[0] = built * part_next
+    hidden_patch = jnp.zeros(e_now, hidden.dtype)
+    for src_i in [*range(part_next)]:
+        clean = lax.dynamic_slice_in_dim(hidden, (odd ^ src_i) * main, main, axis=1)
+        if src_i:
+            clean = ppermute(clean, "seq", [(no, no ^ src_i) for no in range(part_next)])
+        hidden_patch = lax.dynamic_update_slice_in_dim(
+            hidden_patch, clean, (odd ^ src_i) * built, axis=0
+        )
     normed, normal_form, inverse = layer_norm(hidden_patch, modulation)
     projected = jnp.einsum(
         "fpd,dc->fpc",

time: 138 us -> 132 us (0.957)
  starting transfers between devices: 16.2 us -> 33.2 us
  waiting for transfers between devices: 54.1 us -> 40 us
  other arithmetic: 13.2 us -> 8.93 us
  local copies, waits for them, and re-layouts: 18.4 us -> 14.4 us
    ppermute x0 -> x15, starting transfers between devices: none -> 23.2 us  [shards(): ppermute(clean, 'seq', [(no, no ^ src_i) for no in range(part_next)])]
    all_to_all x1 -> x0, waiting for transfers between devices: 19.4 us -> none  [shards(): lax.all_to_all(hidden, 'seq', split_axis=1, concat_axis=0, tiled=True)]
    ppermute x0 -> x15, waiting for transfers between devices: none -> 11.5 us  [shards(): ppermute(clean, 'seq', [(no, no ^ src_i) for no in range(part_next)])]
    all_to_all x1, waiting for transfers between devices: 9.12 us -> 0.01 us  [shards(): lax.all_to_all(temporal_out_grad, 'seq', split_axis=1, concat_axis=0, til...]
    all_to_all x1 -> x0, starting transfers between devices: 4.79 us -> none  [shards(): lax.all_to_all(hidden, 'seq', split_axis=1, concat_axis=0, tiled=True)]
    unnamed x3 -> x2, other arithmetic: 7.44 us -> 3.22 us
    unnamed x32 -> x29, local copies, waits for them, and re-layouts: 9.62 us -> 6.22 us
    all_gather x1, waiting for transfers between devices: 10.7 us -> 12.3 us  [shards(): lax.all_gather(temporal_weights, 'seq', axis=0, tiled=True)]
  transfers between devices with their start and end apart: 5 -> 19, of which waited for: 4 -> 7; matrix products, arithmetic and copies ran while one was open for 33% -> 29% of each run, Pallas kernels for 0% -> 0%
where the time goes in v1:
time: 132 us
  waiting for transfers between devices  40 us (30%)
  starting transfers between devices  33.2 us (25%)
  matrix products  20.4 us (15%)
  between operations  14.7 us (11%)
  local copies, waits for them, and re-layouts  14.4 us (11%)
  other arithmetic  8.93 us (7%)
    ppermute x15, starting transfers between devices, shards(): ppermute(clean, 'seq', [(no, no ^ src_i) for no in range(part_next)])  23.2 us
    all_gather x1, waiting for transfers between devices, shards(): lax.all_gather(spatial_weights, 'seq', axis=0, tiled=True)  14.7 us
    all_gather x1, waiting for transfers between devices, shards(): lax.all_gather(temporal_weights, 'seq', axis=0, tiled=True)  12.3 us
    ppermute x15, waiting for transfers between devices, shards(): ppermute(clean, 'seq', [(no, no ^ src_i) for no in range(part_next)])  11.5 us
    unnamed x29, local copies, waits for them, and re-layouts  6.22 us
    all_to_all x1, starting transfers between devices, shards(): lax.all_to_all(temporal_out_grad, 'seq', split_axis=1, concat_axis=0, til...  6.09 us
    sub x2, matrix products, attend_grad(): attention = jax.nn.softmax(scores, axis=-1)  4.16 us
    all_to_all x1, starting transfers between devices, shards(): lax.all_to_all(branch, 'seq', split_axis=0, concat_axis=1, tiled=True)  3.83 us
  transfers between devices with their start and end apart: 19, of which 7 were waited for; matrix products, arithmetic and copies ran while one was open for 29% of the time, Pallas kernels for 0%

profile of v1, /device:TPU:0, one launch (start us, length us, event | category | flops | bytes accessed | tf_op | source)
XLA Modules:
  0.0 131.7 jit_solution(8852103171129714610)
XLA Ops:
  7.2 0.7 all-gather.4.cloned.1.call-update
  8.3 0.5 collective-permute-start
  8.8 2.6 %collective-permute-start.1 = (bf16[1,16,1152]{2,1,0:T(8,128)(2,1)S(1)}, bf16[1,16,1152]{2,1,0:T(8,128)(2,1)S(1)}, u32[]{:S(2)}, u32[]{:S(2)}) collective-permute-start(bf16[1,16,1152]{2,1,0:T(8,128)(2,1)S(1)} %get-tuple-element.22), channel_id=1, source_target_pairs={{0,2},{1,3},{2,0},{3,1},{4,6},{5,7},{6,4},{7,5},{8,10},{9,11},{10,... | collective-permute-start | bytes 110600 | tf_op jit(solution)/shard_map/ppermute | solution.py:109
  11.5 1.8 %collective-permute-start.3 = (bf16[1,16,1152]{2,1,0:T(8,128)(2,1)S(1)}, bf16[1,16,1152]{2,1,0:T(8,128)(2,1)S(1)}, u32[]{:S(2)}, u32[]{:S(2)}) collective-permute-start(bf16[1,16,1152]{2,1,0:T(8,128)(2,1)S(1)} %get-tuple-element.20), channel_id=1, source_target_pairs={{0,4},{1,5},{2,6},{3,7},{4,0},{5,1},{6,2},{7,3},{8,12},{9,13},{10,... | collective-permute-start | bytes 110600 | tf_op jit(solution)/shard_map/ppermute | solution.py:109
  13.3 0.6 copy.39
  13.9 0.5 broadcast.84
  14.4 2.7 %reduce.10 = bf16[256,576]{1,0:T(8,128)(2,1)S(1)} reduce(bf16[256,1,576]{2,1,0:T(2,128)(2,1)S(1)} %bitcast.93, bf16[]{:T(256)} %broadcast.84), dimensions={1}, to_apply=%bitcast.72.reduce_sub_computation | reduce | bytes 589826
  17.1 1.1 reshape.159
  18.2 6.1 %all-to-all-start = ((bf16[16,2,4608]{2,1,0:T(2,128)(2,1)}), bf16[16,2,4608]{2,1,0:T(2,128)(2,1)S(1)}, u32[]{:S(2)}, u32[]{:S(2)}) async-start(bf16[16,2,4608]{2,1,0:T(2,128)(2,1)} %reshape.159), calls=%async_computation | async-start | bytes 589824 | tf_op jit(solution)/shard_map/all_to_all | solution.py:96
  24.3 0.7 all-gather.6.cloned.1.call-update
  25.2 2.9 %collective-permute-start.5 = (bf16[1,16,1152]{2,1,0:T(8,128)(2,1)S(1)}, bf16[1,16,1152]{2,1,0:T(8,128)(2,1)S(1)}, u32[]{:S(2)}, u32[]{:S(2)}) collective-permute-start(bf16[1,16,1152]{2,1,0:T(8,128)(2,1)S(1)} %get-tuple-element.18), channel_id=1, source_target_pairs={{0,6},{1,7},{2,4},{3,5},{4,2},{5,3},{6,0},{7,1},{8,14},{9,15},{10,... | collective-permute-start | bytes 110600 | tf_op jit(solution)/shard_map/ppermute | solution.py:109
  28.2 2.4 %collective-permute-start.7 = (bf16[1,16,1152]{2,1,0:T(8,128)(2,1)S(1)}, bf16[1,16,1152]{2,1,0:T(8,128)(2,1)S(1)}, u32[]{:S(2)}, u32[]{:S(2)}) collective-permute-start(bf16[1,16,1152]{2,1,0:T(8,128)(2,1)S(1)} %get-tuple-element.16), channel_id=1, source_target_pairs={{0,8},{1,9},{2,10},{3,11},{4,12},{5,13},{6,14},{7,15},{8,0},{9,1},... | collective-permute-start | bytes 110600 | tf_op jit(solution)/shard_map/ppermute | solution.py:109
  30.6 0.3 collective-permute-start.8
  31.0 3.6 %collective-permute-start.9 = (bf16[1,16,1152]{2,1,0:T(8,128)(2,1)S(1)}, bf16[1,16,1152]{2,1,0:T(8,128)(2,1)S(1)}, u32[]{:S(2)}, u32[]{:S(2)}) collective-permute-start(bf16[1,16,1152]{2,1,0:T(8,128)(2,1)S(1)} %get-tuple-element.14), channel_id=1, source_target_pairs={{0,10},{1,11},{2,8},{3,9},{4,14},{5,15},{6,12},{7,13},{8,2},{9,3},... | collective-permute-start | bytes 110600 | tf_op jit(solution)/shard_map/ppermute | solution.py:109
  34.6 2.5 %collective-permute-done.5 = bf16[1,16,1152]{2,1,0:T(8,128)(2,1)S(1)} collective-permute-done((bf16[1,16,1152]{2,1,0:T(8,128)(2,1)S(1)}, bf16[1,16,1152]{2,1,0:T(8,128)(2,1)S(1)}, u32[]{:S(2)}, u32[]{:S(2)}) %collective-permute-start.5) | collective-permute-done | bytes 36896 | tf_op jit(solution)/shard_map/ppermute | solution.py:109
  37.1 3.4 %collective-permute-start.10 = (bf16[1,16,1152]{2,1,0:T(8,128)(2,1)S(1)}, bf16[1,16,1152]{2,1,0:T(8,128)(2,1)S(1)}, u32[]{:S(2)}, u32[]{:S(2)}) collective-permute-start(bf16[1,16,1152]{2,1,0:T(8,128)(2,1)S(1)} %get-tuple-element.13), channel_id=1, source_target_pairs={{0,11},{1,10},{2,9},{3,8},{4,15},{5,14},{6,13},{7,12},{8,3},{9,2},... | collective-permute-start | bytes 110600 | tf_op jit(solution)/shard_map/ppermute | solution.py:109
  40.5 0.5 collective-permute-start.11
  41.1 3.1 %collective-permute-done.7 = bf16[1,16,1152]{2,1,0:T(8,128)(2,1)S(1)} collective-permute-done((bf16[1,16,1152]{2,1,0:T(8,128)(2,1)S(1)}, bf16[1,16,1152]{2,1,0:T(8,128)(2,1)S(1)}, u32[]{:S(2)}, u32[]{:S(2)}) %collective-permute-start.7) | collective-permute-done | bytes 36896 | tf_op jit(solution)/shard_map/ppermute | solution.py:109
  44.2 0.8 collective-permute-start.12
  45.0 3.1 %collective-permute-start.13 = (bf16[1,16,1152]{2,1,0:T(8,128)(2,1)S(1)}, bf16[1,16,1152]{2,1,0:T(8,128)(2,1)S(1)}, u32[]{:S(2)}, u32[]{:S(2)}) collective-permute-start(bf16[1,16,1152]{2,1,0:T(8,128)(2,1)S(1)} %get-tuple-element.25), channel_id=1, source_target_pairs={{0,14},{1,15},{2,12},{3,13},{4,10},{5,11},{6,8},{7,9},{8,6},{9,7},... | collective-permute-start | bytes 110600 | tf_op jit(solution)/shard_map/ppermute | solution.py:109
  48.2 1.0 collective-permute-start.14
  49.3 0.3 collective-permute-done.12
  49.6 2.7 %collective-permute-done.13 = bf16[1,16,1152]{2,1,0:T(8,128)(2,1)S(1)} collective-permute-done((bf16[1,16,1152]{2,1,0:T(8,128)(2,1)S(1)}, bf16[1,16,1152]{2,1,0:T(8,128)(2,1)S(1)}, u32[]{:S(2)}, u32[]{:S(2)}) %collective-permute-start.13) | collective-permute-done | bytes 36896 | tf_op jit(solution)/shard_map/ppermute | solution.py:109
  52.3 2.9 %collective-permute-done.14 = bf16[1,16,1152]{2,1,0:T(8,128)(2,1)S(1)} collective-permute-done((bf16[1,16,1152]{2,1,0:T(8,128)(2,1)S(1)}, bf16[1,16,1152]{2,1,0:T(8,128)(2,1)S(1)}, u32[]{:S(2)}, u32[]{:S(2)}) %collective-permute-start.14) | collective-permute-done | bytes 36896 | tf_op jit(solution)/shard_map/ppermute | solution.py:109
  55.2 0.2 convert_reduce_fusion
  55.3 0.3 fusion.36
  55.6 0.8 reshape.160
  56.4 1.8 %bitcast_reduce_fusion = bf16[256,576]{1,0:T(8,128)(2,1)S(1)} fusion(bf16[256,1,576]{2,1,0:T(2,128)(2,1)S(1)} %reshape.160), kind=kLoop, calls=%fused_computation.114 | loop fusion | bytes 589824 | tf_op jit(solution)/shard_map/all_to_all | solution.py:96
  58.3 0.6 reshape.139
  58.8 12.3 %all-gather.4.cloned.1.call-done = bf16[1152,1728]{1,0:T(8,128)(2,1)} async-done(((bf16[72,1728]{1,0:T(8,128)(2,1)}), bf16[1152,1728]{1,0:T(8,128)(2,1)}) %all-gather.4.cloned.1.call-update) | async-done | bytes 3981328 | tf_op jit(solution)/shard_map/all_gather | solution.py:117
  71.2 3.6 %fusion.9 = bf16[16,16,1728]{2,1,0:T(8,128)(2,1)S(1)} fusion(bf16[1152,1728]{1,0:T(8,128)(2,1)} %all-gather.4.cloned.1.call-done, bf16[16,16,1152]{2,1,0:T(8,128)(2,1)S(1)} %constant_dynamic-update-slice_fusion.14, f32[1152]{0:T(1024)S(1)} %broadcast_add_fusion, f32[16,16]{1,0:T(8,128)S(1)} %add_rsqrt_fusion, f32[16,16]{1,0:T(8,128)S(1)} %broadcast_multiply_fusion.2), kind=kOutput, calls=%fused_computation.7 | convolution fusion | flops 1021132800 | bytes 5462528 | tf_op jit(solution)/shard_map/fpd,dc->fpc/dot_general | solution.py:114
  74.8 0.2 fusion.69
  75.0 0.6 reshape.136
  75.5 0.6 reshape.137
  76.1 2.0 %fusion.71 = (f32[16,8,16]{2,1,0:T(8,128)S(1)}, f32[16,8,16,16]{2,3,1,0:T(8,128)}) fusion(bf16[16,16,8,72]{3,2,1,0:T(8,128)(2,1)S(1)} %reshape.136, bf16[16,16,8,72]{3,2,1,0:T(8,128)(2,1)S(1)} %reshape.137), kind=kOutput, calls=%fused_computation.112 | convolution fusion | flops 4816911 | bytes 729088 | tf_op jit(solution)/shard_map/sub | solution.py:22
  78.1 1.7 %fusion.27 = bf16[16,16,8,72]{3,0,2,1:T(8,128)(2,1)S(1)} fusion(bf16[16,16,8,72]{3,2,1,0:T(8,128)(2,1)S(1)} %reshape.139, f32[16,8,16,16]{2,3,1,0:T(8,128)} %get-tuple-element.27, f32[16,8,16]{2,1,0:T(8,128)S(1)} %get-tuple-element.26), kind=kOutput, calls=%fused_computation.37 | convolution fusion | flops 4931584 | bytes 729088 | tf_op jit(solution)/shard_map/bhlm,lbhd->mbhd/dot_general | solution.py:38
  80.0 0.4 reshape.142
  80.4 0.6 reshape.138
  80.9 1.7 %convolution_bitcast_fusion = f32[16,8,16,72]{3,2,1,0:T(8,128)S(1)} fusion(bf16[16,16,8,72]{3,2,1,0:T(8,128)(2,1)S(1)} %reshape.138, f32[16,8,16,16]{2,3,1,0:T(8,128)} %get-tuple-element.27, f32[16,8,16]{2,1,0:T(8,128)} %copy-done.11), kind=kOutput, calls=%fused_computation.23 | convolution fusion | flops 4784128 | bytes 1024000 | tf_op jit(solution)/shard_map/bhlm,mbhd->lbhd/dot_general | solution.py:24
  82.6 0.5 multiply_reduce_fusion.1
  83.2 0.7 copy.63
  83.9 2.0 %fusion.22 = bf16[16,8,16,16]{2,3,1,0:T(8,128)(2,1)S(1)} fusion(f32[16,8,16]{2,1,0:T(8,128)} %copy.63, bf16[16,16,8,72]{3,2,1,0:T(8,128)(2,1)S(1)} %reshape.139, bf16[16,16,8,72]{3,2,1,0:T(8,128)(2,1)S(1)} %reshape.138, f32[16,8,16,16]{2,3,1,0:T(8,128)} %get-tuple-element.27, f32[16,8,16]{2,1,0:T(8,128)} %copy-done.11), kind=kOutput, calls=%fused_computation.28 | convolution fusion | flops 4849664 | bytes 802816 | tf_op jit(solution)/shard_map/lbhd,mbhd->bhlm/dot_general | solution.py:28
  85.9 0.4 fusion.25
  86.5 0.4 reshape.141
  86.8 0.5 fusion.26
  87.5 0.4 reshape.140
  87.9 0.7 concatenate.3
  88.5 3.7 %fusion.68 = (f32[16,16]{1,0:T(8,128)S(1)}, f32[16,16]{1,0:T(8,128)S(1)}, f32[16,16,1152]{2,1,0:T(8,128)S(1)}) fusion(f32[16,16]{1,0:T(8,128)S(1)} %add_rsqrt_fusion, f32[16,16]{1,0:T(8,128)S(1)} %broadcast_multiply_fusion.2, bf16[16,16,1152]{2,1,0:T(8,128)(2,1)S(1)} %constant_dynamic-update-slice_fusion.14, f32[1152]{0:T(1024)S(1)} %copy-done.10, ...), kind=kOutput, calls=%fused_computation.109 | convolution fusion | flops 1021279744 | bytes 6644224 | tf_op jit(solution)/shard_map/fpc,dc->fpd/dot_general | solution.py:122
  92.2 1.2 fusion.35
  93.4 3.8 %all-to-all-start.1 = ((bf16[16,16,1152]{2,1,0:T(8,128)(2,1)}), bf16[16,16,1152]{2,1,0:T(8,128)(2,1)S(1)}, u32[]{:S(2)}, u32[]{:S(2)}) async-start(bf16[16,16,1152]{2,1,0:T(8,128)(2,1)} %fusion.35), calls=%async_computation.1 | async-start | bytes 1179648 | tf_op jit(solution)/shard_map/all_to_all | solution.py:132
  97.3 0.8 fusion.70
  98.0 2.2 %fusion.76 = (f32[8,256]{1,0:T(8,128)S(1)}, f32[8,256,256]{1,2,0:T(8,128)}) fusion(bf16[256,8,72]{0,2,1:T(8,128)(2,1)S(1)} %bitcast.95, bf16[256,8,72]{0,2,1:T(8,128)(2,1)S(1)} %bitcast.97), kind=kOutput, calls=%fused_computation.113 | convolution fusion | flops 77070592 | bytes 2695168 | tf_op jit(solution)/shard_map/sub | solution.py:22
  100.2 1.8 %fusion.38 = bf16[8,256,256]{1,2,0:T(8,128)(2,1)S(1)} fusion(f32[8,256,256]{1,2,0:T(8,128)} %get-tuple-element.30, f32[8,256]{1,0:T(8,128)S(1)} %get-tuple-element.29), kind=kLoop, calls=%fused_computation.54 | loop fusion | flops 1048576 | bytes 3153920 | tf_op jit(solution)/shard_map/convert_element_type | solution.py:23
  102.0 14.7 %all-gather.6.cloned.1.call-done = bf16[16,36,1152]{2,1,0:T(8,128)(2,1)} async-done(((bf16[1,36,1152]{2,1,0:T(8,128)(2,1)}), bf16[16,36,1152]{2,1,0:T(8,128)(2,1)}) %all-gather.6.cloned.1.call-update) | async-done | bytes 1327120 | tf_op jit(solution)/shard_map/all_gather | solution.py:140
  116.8 2.2 %reshape.150 = bf16[576,1152]{1,0:T(8,128)(2,1)S(1)} reshape(bf16[16,36,1152]{2,1,0:T(8,128)(2,1)} %all-gather.6.cloned.1.call-done) | data formatting | bytes 2654208
  119.0 1.2 add_convert_fusion
  120.3 0.6 convolution_convert_fusion.1
  120.9 0.3 fusion.30
  121.2 0.9 copy-done
  122.1 0.5 multiply_convert_fusion
  122.6 0.3 fusion.28
  122.9 0.5 fusion.29
  123.4 0.4 convolution_convert_fusion.2
  123.8 1.0 pad_maximum_fusion
  (64 shorter events, 1.2 us)
Async XLA Ops:
  7.2 1.1 copy-start.4
  7.2 6.1 %copy-start.5 = (bf16[1,256,576]{1,2,0:T(8,128)(2,1)S(1)}, bf16[1,256,576]{1,2,0:T(8,128)(2,1)}, u32[]{:S(2)}) copy-start(bf16[1,256,576]{1,2,0:T(8,128)(2,1)} %param.9) | copy-start | bytes 884740
  7.2 64.0 %all-gather.4.cloned.1.call-start = ((), (), s32[]{:S(2)}) async-start(), calls=%async_computation.2 | async-start | bytes 4386816 | tf_op jit(solution)/shard_map/all_gather | solution.py:117
  8.3 16.9 %collective-permute-start = (bf16[1,16,1152]{2,1,0:T(8,128)(2,1)S(1)}, bf16[1,16,1152]{2,1,0:T(8,128)(2,1)S(1)}, u32[]{:S(2)}, u32[]{:S(2)}) collective-permute-start(bf16[1,16,1152]{2,1,0:T(8,128)(2,1)S(1)} %get-tuple-element.23), channel_id=1, source_target_pairs={{0,1},{1,0},{2,3},{3,2},{4,5},{5,4},{6,7},{7,6},{8,9},{9,8},{10,11... | collective-permute-start | bytes 110600 | tf_op jit(solution)/shard_map/ppermute | solution.py:109
  8.8 19.3 %collective-permute-start.1 = (bf16[1,16,1152]{2,1,0:T(8,128)(2,1)S(1)}, bf16[1,16,1152]{2,1,0:T(8,128)(2,1)S(1)}, u32[]{:S(2)}, u32[]{:S(2)}) collective-permute-start(bf16[1,16,1152]{2,1,0:T(8,128)(2,1)S(1)} %get-tuple-element.22), channel_id=1, source_target_pairs={{0,2},{1,3},{2,0},{3,1},{4,6},{5,7},{6,4},{7,5},{8,10},{9,11},{10,... | collective-permute-start | bytes 110600 | tf_op jit(solution)/shard_map/ppermute | solution.py:109
  11.4 16.8 %collective-permute-start.2 = (bf16[1,16,1152]{2,1,0:T(8,128)(2,1)S(1)}, bf16[1,16,1152]{2,1,0:T(8,128)(2,1)S(1)}, u32[]{:S(2)}, u32[]{:S(2)}) collective-permute-start(bf16[1,16,1152]{2,1,0:T(8,128)(2,1)S(1)} %get-tuple-element.21), channel_id=1, source_target_pairs={{0,3},{1,2},{2,1},{3,0},{4,7},{5,6},{6,5},{7,4},{8,11},{9,10},{10,... | collective-permute-start | bytes 110600 | tf_op jit(solution)/shard_map/ppermute | solution.py:109
  11.5 19.2 %collective-permute-start.3 = (bf16[1,16,1152]{2,1,0:T(8,128)(2,1)S(1)}, bf16[1,16,1152]{2,1,0:T(8,128)(2,1)S(1)}, u32[]{:S(2)}, u32[]{:S(2)}) collective-permute-start(bf16[1,16,1152]{2,1,0:T(8,128)(2,1)S(1)} %get-tuple-element.20), channel_id=1, source_target_pairs={{0,4},{1,5},{2,6},{3,7},{4,0},{5,1},{6,2},{7,3},{8,12},{9,13},{10,... | collective-permute-start | bytes 110600 | tf_op jit(solution)/shard_map/ppermute | solution.py:109
  13.3 17.7 %collective-permute-start.4 = (bf16[1,16,1152]{2,1,0:T(8,128)(2,1)S(1)}, bf16[1,16,1152]{2,1,0:T(8,128)(2,1)S(1)}, u32[]{:S(2)}, u32[]{:S(2)}) collective-permute-start(bf16[1,16,1152]{2,1,0:T(8,128)(2,1)S(1)} %get-tuple-element.19), channel_id=1, source_target_pairs={{0,5},{1,4},{2,7},{3,6},{4,1},{5,0},{6,3},{7,2},{8,13},{9,12},{10,... | collective-permute-start | bytes 110600 | tf_op jit(solution)/shard_map/ppermute | solution.py:109
  13.9 11.2 %copy-start.8 = (f32[1152]{0:T(1024)S(1)}, f32[1152]{0:T(1024)}, u32[]{:S(2)}) copy-start(f32[1152]{0:T(1024)} %param.11) | copy-start | bytes 13828
  18.2 37.5 %all-to-all-start = ((bf16[16,2,4608]{2,1,0:T(2,128)(2,1)}), bf16[16,2,4608]{2,1,0:T(2,128)(2,1)S(1)}, u32[]{:S(2)}, u32[]{:S(2)}) async-start(bf16[16,2,4608]{2,1,0:T(2,128)(2,1)} %reshape.159), calls=%async_computation | async-start | bytes 589824 | tf_op jit(solution)/shard_map/all_to_all | solution.py:96
  24.3 92.5 %all-gather.6.cloned.1.call-start = ((), (), s32[]{:S(2)}) async-start(), calls=%async_computation.3 | async-start | bytes 1566720 | tf_op jit(solution)/shard_map/all_gather | solution.py:140
  25.1 46.1 %copy-start.9 = (f32[1152]{0:T(1024)}, f32[1152]{0:T(1024)S(1)}, u32[]{:S(2)}) copy-start(f32[1152]{0:T(1024)S(1)} %broadcast_add_fusion) | copy-start | bytes 13828
  25.2 11.9 %collective-permute-start.5 = (bf16[1,16,1152]{2,1,0:T(8,128)(2,1)S(1)}, bf16[1,16,1152]{2,1,0:T(8,128)(2,1)S(1)}, u32[]{:S(2)}, u32[]{:S(2)}) collective-permute-start(bf16[1,16,1152]{2,1,0:T(8,128)(2,1)S(1)} %get-tuple-element.18), channel_id=1, source_target_pairs={{0,6},{1,7},{2,4},{3,5},{4,2},{5,3},{6,0},{7,1},{8,14},{9,15},{10,... | collective-permute-start | bytes 110600 | tf_op jit(solution)/shard_map/ppermute | solution.py:109
  28.1 12.4 %collective-permute-start.6 = (bf16[1,16,1152]{2,1,0:T(8,128)(2,1)S(1)}, bf16[1,16,1152]{2,1,0:T(8,128)(2,1)S(1)}, u32[]{:S(2)}, u32[]{:S(2)}) collective-permute-start(bf16[1,16,1152]{2,1,0:T(8,128)(2,1)S(1)} %get-tuple-element.17), channel_id=1, source_target_pairs={{0,7},{1,6},{2,5},{3,4},{4,3},{5,2},{6,1},{7,0},{8,15},{9,14},{10,... | collective-permute-start | bytes 110600 | tf_op jit(solution)/shard_map/ppermute | solution.py:109
  28.2 16.0 %collective-permute-start.7 = (bf16[1,16,1152]{2,1,0:T(8,128)(2,1)S(1)}, bf16[1,16,1152]{2,1,0:T(8,128)(2,1)S(1)}, u32[]{:S(2)}, u32[]{:S(2)}) collective-permute-start(bf16[1,16,1152]{2,1,0:T(8,128)(2,1)S(1)} %get-tuple-element.16), channel_id=1, source_target_pairs={{0,8},{1,9},{2,10},{3,11},{4,12},{5,13},{6,14},{7,15},{8,0},{9,1},... | collective-permute-start | bytes 110600 | tf_op jit(solution)/shard_map/ppermute | solution.py:109
  30.6 14.3 %collective-permute-start.8 = (bf16[1,16,1152]{2,1,0:T(8,128)(2,1)S(1)}, bf16[1,16,1152]{2,1,0:T(8,128)(2,1)S(1)}, u32[]{:S(2)}, u32[]{:S(2)}) collective-permute-start(bf16[1,16,1152]{2,1,0:T(8,128)(2,1)S(1)} %get-tuple-element.15), channel_id=1, source_target_pairs={{0,9},{1,8},{2,11},{3,10},{4,13},{5,12},{6,15},{7,14},{8,1},{9,0},... | collective-permute-start | bytes 110600 | tf_op jit(solution)/shard_map/ppermute | solution.py:109
  31.0 17.2 %collective-permute-start.9 = (bf16[1,16,1152]{2,1,0:T(8,128)(2,1)S(1)}, bf16[1,16,1152]{2,1,0:T(8,128)(2,1)S(1)}, u32[]{:S(2)}, u32[]{:S(2)}) collective-permute-start(bf16[1,16,1152]{2,1,0:T(8,128)(2,1)S(1)} %get-tuple-element.14), channel_id=1, source_target_pairs={{0,10},{1,11},{2,8},{3,9},{4,14},{5,15},{6,12},{7,13},{8,2},{9,3},... | collective-permute-start | bytes 110600 | tf_op jit(solution)/shard_map/ppermute | solution.py:109
  37.1 12.1 %collective-permute-start.10 = (bf16[1,16,1152]{2,1,0:T(8,128)(2,1)S(1)}, bf16[1,16,1152]{2,1,0:T(8,128)(2,1)S(1)}, u32[]{:S(2)}, u32[]{:S(2)}) collective-permute-start(bf16[1,16,1152]{2,1,0:T(8,128)(2,1)S(1)} %get-tuple-element.13), channel_id=1, source_target_pairs={{0,11},{1,10},{2,9},{3,8},{4,15},{5,14},{6,13},{7,12},{8,3},{9,2},... | collective-permute-start | bytes 110600 | tf_op jit(solution)/shard_map/ppermute | solution.py:109
  40.5 8.7 %collective-permute-start.11 = (bf16[1,16,1152]{2,1,0:T(8,128)(2,1)S(1)}, bf16[1,16,1152]{2,1,0:T(8,128)(2,1)S(1)}, u32[]{:S(2)}, u32[]{:S(2)}) collective-permute-start(bf16[1,16,1152]{2,1,0:T(8,128)(2,1)S(1)} %get-tuple-element.12), channel_id=1, source_target_pairs={{0,12},{1,13},{2,14},{3,15},{4,8},{5,9},{6,10},{7,11},{8,4},{9,5},... | collective-permute-start | bytes 110600 | tf_op jit(solution)/shard_map/ppermute | solution.py:109
  44.2 5.3 %collective-permute-start.12 = (bf16[1,16,1152]{2,1,0:T(8,128)(2,1)S(1)}, bf16[1,16,1152]{2,1,0:T(8,128)(2,1)S(1)}, u32[]{:S(2)}, u32[]{:S(2)}) collective-permute-start(bf16[1,16,1152]{2,1,0:T(8,128)(2,1)S(1)} %get-tuple-element.11), channel_id=1, source_target_pairs={{0,13},{1,12},{2,15},{3,14},{4,9},{5,8},{6,11},{7,10},{8,5},{9,4},... | collective-permute-start | bytes 110600 | tf_op jit(solution)/shard_map/ppermute | solution.py:109
  45.0 7.3 %collective-permute-start.13 = (bf16[1,16,1152]{2,1,0:T(8,128)(2,1)S(1)}, bf16[1,16,1152]{2,1,0:T(8,128)(2,1)S(1)}, u32[]{:S(2)}, u32[]{:S(2)}) collective-permute-start(bf16[1,16,1152]{2,1,0:T(8,128)(2,1)S(1)} %get-tuple-element.25), channel_id=1, source_target_pairs={{0,14},{1,15},{2,12},{3,13},{4,10},{5,11},{6,8},{7,9},{8,6},{9,7},... | collective-permute-start | bytes 110600 | tf_op jit(solution)/shard_map/ppermute | solution.py:109
  48.2 7.0 %collective-permute-start.14 = (bf16[1,16,1152]{2,1,0:T(8,128)(2,1)S(1)}, bf16[1,16,1152]{2,1,0:T(8,128)(2,1)S(1)}, u32[]{:S(2)}, u32[]{:S(2)}) collective-permute-start(bf16[1,16,1152]{2,1,0:T(8,128)(2,1)S(1)} %get-tuple-element.10), channel_id=1, source_target_pairs={{0,15},{1,14},{2,13},{3,12},{4,11},{5,10},{6,9},{7,8},{8,7},{9,6},... | collective-permute-start | bytes 110600 | tf_op jit(solution)/shard_map/ppermute | solution.py:109
  78.1 1.8 %copy-start.11 = (f32[16,8,16]{2,1,0:T(8,128)}, f32[16,8,16]{2,1,0:T(8,128)S(1)}, u32[]{:S(2)}) copy-start(f32[16,8,16]{2,1,0:T(8,128)S(1)} %get-tuple-element.26) | copy-start | bytes 24580
  87.5 1.1 copy-start.10
  93.4 3.8 %copy-start.2 = (bf16[3,1,256,576]{2,3,1,0:T(8,128)(2,1)S(1)}, bf16[3,1,256,576]{2,3,1,0:T(8,128)(2,1)}, u32[]{:S(2)}) copy-start(bf16[3,1,256,576]{2,3,1,0:T(8,128)(2,1)} %param.7) | copy-start | bytes 2654212
  93.4 25.6 %all-to-all-start.1 = ((bf16[16,16,1152]{2,1,0:T(8,128)(2,1)}), bf16[16,16,1152]{2,1,0:T(8,128)(2,1)S(1)}, u32[]{:S(2)}, u32[]{:S(2)}) async-start(bf16[16,16,1152]{2,1,0:T(8,128)(2,1)} %fusion.35), calls=%async_computation.1 | async-start | bytes 1179648 | tf_op jit(solution)/shard_map/all_to_all | solution.py:132
  100.2 1.8 %copy-start.6 = (f32[8,256]{1,0:T(8,128)}, f32[8,256]{1,0:T(8,128)S(1)}, u32[]{:S(2)}) copy-start(f32[8,256]{1,0:T(8,128)S(1)} %get-tuple-element.29) | copy-start | bytes 24580
  119.0 1.9 %copy-start.1 = (bf16[1,1,256,576]{2,3,1,0:T(8,128)(2,1)S(1)}, bf16[1,1,256,576]{2,3,1,0:T(8,128)(2,1)}, u32[]{:S(2)}) copy-start(bf16[1,1,256,576]{2,3,1,0:T(8,128)(2,1)} %get-tuple-element.7) | copy-start | bytes 884740
  120.3 1.0 copy-start.3
  120.3 1.8 %copy-start = (f32[8,256,256]{1,2,0:T(8,128)S(1)}, f32[8,256,256]{1,2,0:T(8,128)}, u32[]{:S(2)}) copy-start(f32[8,256,256]{1,2,0:T(8,128)} %get-tuple-element.30) | copy-start | bytes 6291460
  120.9 1.2 copy-start.7
Sparse Core Ops, SparseCore 0:
  10.3 60.7 all-gather.3
  73.3 43.4 all-gather.5
